TPU v7x, 32 devices: a whole 2x2x4 slice. The times are simulated.
32 devices in a mesh: groups: 2 (over y), tm: 4 (over z), weights: 2 (over core), batch: 2 (over x).
Axes of the slice: x: 2, y: 2, z: 4, core: 2. Of those that a mesh axis runs over, the one named last changes fastest.
Arguments:
- clip_feats: float32 [16, 8192, 128], P(('groups', 'weights', 'batch'), 'tm'), parts along dimension 0, may hold values from -6 to 6
- teacher: float32 [16, 4096, 256], P(('groups', 'weights', 'batch'), 'tm'), parts along dimension 0, may hold values from -6 to 6
- starts: int32 [16], P('groups'), parts along dimension 0, may hold values from 0 to 1023
- lengths: int32 [16], P('groups'), parts along dimension 0, may hold values from 2048 to 3072
- dilated_weight: float32 [7, 128, 128], replicated, may hold values from -0.1875 to 0.1875
- dilated_bias: float32 [128], replicated, may hold values from -0.5 to 0.5
- mix_w: float32 [128, 128], replicated, may hold values from -0.5 to 0.5
- mix_b: float32 [128], replicated, may hold values from -0.5 to 0.5
- down_w: float32 [4, 128, 256], replicated, may hold values from -0.25 to 0.25
- down_b: float32 [256], replicated, may hold values from -0.5 to 0.5
Outputs:
- grad_conv: float32 [14, 128, 128], P('groups', None, 'weights'), parts along dimension 0
- grad_conv_bias: float32 [256], P(('groups', 'weights')), parts along dimension 0
- grad_mix: float32 [256, 128], P(('groups', 'weights')), parts along dimension 0
- grad_mix_bias: float32 [256], P(('groups', 'weights')), parts along dimension 0
- grad_down: float32 [8, 128, 256], P('groups', None, 'weights'), parts along dimension 0
- grad_down_bias: float32 [512], P(('groups', 'weights')), parts along dimension 0
- loss: float32 [2], P('groups'), parts along dimension 0
There are 2 independent parts, one for each index of `groups`. A program takes and returns all parts, laid end to end along the dimension named above; an argument that names none is the same for every part. Nothing has to cross between parts.
All inputs are finite; a program needn't handle non-finite values.
Results may differ from a plain program's by a relative error of at most 0.0003.
Values sent between devices are 32-bit elements; how exact they have to be, the bound alone decides.
A program may use at most 64 MiB of HBM per device.

v0:
```python
import functools

import jax
import jax.numpy as jnp
from jax import lax
from jax.experimental import pallas as pl
from jax.experimental.pallas import tpu as pltpu
from jax.sharding import PartitionSpec as P

TAPS = 7
RATE = 9
HALO = 32
LEAD = 40
EDGE = 24
CHUNK = 256


def elu(v):
    return jnp.where(v > 0, v, jnp.exp(jnp.minimum(v, 0.0)) - 1.0)


def slope(e):
    return jnp.where(e > 0, 1.0, e + 1.0)


def mm(a, b):
    return lax.dot_general(a, b, (((1,), (0,)), ((), ())), precision=lax.Precision.HIGH,
                           preferred_element_type=jnp.float32)


def mm_t(a, b):
    return lax.dot_general(a, b, (((0,), (0,)), ((), ())), precision=lax.Precision.HIGH,
                           preferred_element_type=jnp.float32)


def local_kernel(
    bounds, x, xl, xr, te, tl, tr, wc, bc, wm, bm, wd, bd,
    o_conv, o_mix, o_down, o_bias,
    act, ya, yb, hid, sec, d0, d1, dsec, dhid, w2, wb, acc2, accd,
):
    step = pl.program_id(0)
    steps = pl.num_programs(0)
    T, C = x.shape[1], x.shape[2]
    N, CO = te.shape[1], te.shape[2]
    t0 = bounds[3] * T
    j0 = bounds[3] * N
    total = bounds[2] * T
    first = bounds[4 + 2 * step]
    last = first + bounds[5 + 2 * step]

    @pl.when(step == 0)
    def _():
        for k in range(TAPS + 1):
            m, p = k // 2, k % 2
            w2[m * C:(m + 1) * C, p * C:(p + 1) * C] = (
                wc[k] if k < TAPS else jnp.zeros((C, C), jnp.float32))
        for k in range(4):
            r, p = k // 2, k % 2
            wb[r * CO:(r + 1) * CO, p * C:(p + 1) * C] = wd[k].T
        acc2[...] = jnp.zeros_like(acc2)
        accd[...] = jnp.zeros_like(accd)
        o_mix[...] = jnp.zeros_like(o_mix)
        o_bias[...] = jnp.zeros_like(o_bias)
        dhid[...] = jnp.zeros_like(dhid)
        act[0:8] = jnp.zeros((8, C), jnp.float32)
        act[LEAD + T + HALO:] = jnp.zeros_like(act[LEAD + T + HALO:])
        sec[0:EDGE] = jnp.zeros((EDGE, C), jnp.float32)
        sec[EDGE + T + 8:] = jnp.zeros_like(sec[EDGE + T + 8:])

    act[8:LEAD] = elu(xl[0])
    act[LEAD + T:LEAD + T + HALO] = elu(xr[0])

    @pl.loop(0, T // CHUNK)
    def _(i):
        s = pl.multiple_of(i * CHUNK, CHUNK)
        act[pl.ds(LEAD + s, CHUNK)] = elu(x[0, pl.ds(s, CHUNK)])

    def conv(t, n):
        a = jnp.concatenate(
            [act[pl.ds(LEAD - 27 + 18 * m + t, n)] for m in range(4)], axis=1)
        r = mm(a, w2[...])
        row = pl.ds(8 + t, n)
        ya[row] = r[:, :C]
        yb[row] = r[:, C:]

    @pl.loop(0, T // CHUNK)
    def _(i):
        conv(i * CHUNK - 8, CHUNK)

    conv(T - 8, 32)

    def section(t, n, xv):
        h = ya[pl.ds(8 + t, n)] + yb[pl.ds(17 + t, n)] + bc[...]
        g = elu(h)
        hid[pl.ds(8 + t, n)] = g
        v = elu(xv + mm(g, wm[...]) + bm[...])
        pos = t0 + t + lax.broadcasted_iota(jnp.int32, (n, C), 0)
        sec[pl.ds(EDGE + t, n)] = jnp.where((pos >= 0) & (pos < total), v, 0.0)

    section(-8, 8, xl[0, HALO - 8:])
    section(T, 8, xr[0, :8])

    @pl.loop(0, T // CHUNK)
    def _(i):
        s = pl.multiple_of(i * CHUNK, CHUNK)
        section(s, CHUNK, x[0, pl.ds(s, CHUNK)])

    def error(j, n, tv):
        a = jnp.concatenate(
            [sec[pl.ds(EDGE + 2 * j + k - 1, n, stride=2)] for k in range(4)], axis=1)
        e = mm(a, wd[...].reshape(4 * C, CO)) + bd[...] - tv
        pos = j0 + j + lax.broadcasted_iota(jnp.int32, (n, CO), 0)
        d = jnp.where((pos >= first) & (pos < last), e, 0.0)
        d0[pl.ds(8 + j, n)] = d[:, :C]
        d1[pl.ds(8 + j, n)] = d[:, C:]
        return a, d

    error(-8, 8, tl[0])
    error(N, 8, tr[0])

    @pl.loop(0, N // CHUNK)
    def _(i):
        s = pl.multiple_of(i * CHUNK, CHUNK)
        a, d = error(s, CHUNK, te[0, pl.ds(s, CHUNK)])
        accd[...] += mm_t(a, d)
        o_bias[0:1, :] += jnp.sum(d, axis=0, keepdims=True)
        o_bias[1:2, :] += jnp.sum(d * d, axis=0, keepdims=True)

    def back(j, n):
        b = jnp.concatenate(
            [d0[pl.ds(8 + j, n)], d1[pl.ds(8 + j, n)],
             d0[pl.ds(7 + j, n)], d1[pl.ds(7 + j, n)]], axis=1)
        r = mm(b, wb[...])
        dsec[pl.ds(EDGE + 2 * j - 1, n, stride=2)] = r[:, :C]
        dsec[pl.ds(EDGE + 2 * j, n, stride=2)] = r[:, C:]

    @pl.loop(0, N // CHUNK)
    def _(i):
        back(pl.multiple_of(i * CHUNK, CHUNK), CHUNK)

    back(N, 8)

    @pl.loop(0, T // CHUNK)
    def _(i):
        s = pl.multiple_of(i * CHUNK, CHUNK)
        ds = dsec[pl.ds(EDGE + s, CHUNK)] * slope(sec[pl.ds(EDGE + s, CHUNK)])
        g = hid[pl.ds(8 + s, CHUNK)]
        o_mix[...] += mm_t(g, ds)
        dg = lax.dot_general(ds, wm[...], (((1,), (1,)), ((), ())),
                             precision=lax.Precision.HIGH,
                             preferred_element_type=jnp.float32)
        dh = dg * slope(g)
        dhid[pl.ds(16 + s, CHUNK)] = dh
        o_bias[2:3, :C] += jnp.sum(ds, axis=0, keepdims=True)
        o_bias[2:3, C:] += jnp.sum(dh, axis=0, keepdims=True)

    def taps(t, n):
        a = jnp.concatenate(
            [act[pl.ds(LEAD - 27 + 18 * m + t, n)] for m in range(4)], axis=1)
        d = jnp.concatenate(
            [dhid[pl.ds(16 + t, n)], dhid[pl.ds(7 + t, n)]], axis=1)
        acc2[...] += mm_t(a, d)

    @pl.loop(0, T // CHUNK)
    def _(i):
        taps(pl.multiple_of(i * CHUNK, CHUNK), CHUNK)

    taps(T, 16)

    @pl.when(step == steps - 1)
    def _():
        for k in range(TAPS):
            m, p = k // 2, k % 2
            o_conv[k] = acc2[m * C:(m + 1) * C, p * C:(p + 1) * C]
        for k in range(4):
            o_down[k] = accd[k * C:(k + 1) * C]


def local_grads(bounds, x, xl, xr, te, tl, tr, wc, bc, wm, bm, wd, bd):
    B, T, C = x.shape
    N, CO = te.shape[1:]
    f32 = jnp.float32

    def clip(a):
        return pl.BlockSpec((1,) + a.shape[1:], lambda i, *_: (i, 0, 0))

    def whole(a):
        return pl.BlockSpec(a.shape, lambda i, *_: (0,) * len(a.shape))

    outs = [jax.ShapeDtypeStruct(s, f32) for s in
            (wc.shape, wm.shape, wd.shape, (8, CO))]
    return pl.pallas_call(
        local_kernel,
        out_shape=outs,
        grid_spec=pltpu.PrefetchScalarGridSpec(
            num_scalar_prefetch=1,
            grid=(B,),
            in_specs=[clip(a) for a in (x, xl, xr, te, tl, tr)]
            + [whole(a) for a in (wc, bc, wm, bm, wd, bd)],
            out_specs=[whole(o) for o in outs],
            scratch_shapes=[
                pltpu.VMEM((LEAD + T + HALO + 56, C), f32),
                pltpu.VMEM((T + 32, C), f32),
                pltpu.VMEM((T + 32, C), f32),
                pltpu.VMEM((T + 16, C), f32),
                pltpu.VMEM((EDGE + T + 32, C), f32),
                pltpu.VMEM((N + 16, CO // 2), f32),
                pltpu.VMEM((N + 16, CO // 2), f32),
                pltpu.VMEM((EDGE + T + 32, C), f32),
                pltpu.VMEM((T + 32, C), f32),
                pltpu.VMEM((4 * C, 2 * C), f32),
                pltpu.VMEM((2 * CO, 2 * C), f32),
                pltpu.VMEM((4 * C, 2 * C), f32),
                pltpu.VMEM((4 * C, CO), f32),
            ],
        ),
        compiler_params=pltpu.CompilerParams(vmem_limit_bytes=48 * 2**20),
    )(bounds, x, xl, xr, te, tl, tr, wc, bc, wm, bm, wd, bd)


def shift(a, up):
    count = lax.axis_size("tm")
    pairs = [(i, i + 1) if up else (i + 1, i) for i in range(count - 1)]
    return lax.ppermute(a, "tm", pairs)


def shards(x, te, starts, lengths, wc, bc, wm, bm, wd, bd):
    B, T, C = x.shape
    N, CO = te.shape[1:]
    xl = shift(x[:, T - HALO:], True)
    xr = shift(x[:, :HALO], False)
    tl = shift(te[:, N - 8:], True)
    tr = shift(te[:, :8], False)
    mine = lax.axis_index(("weights", "batch")) * B
    own = jnp.stack([lax.dynamic_slice_in_dim(starts, mine, B),
                     lax.dynamic_slice_in_dim(lengths, mine, B)], axis=1).reshape(-1)
    tm = lax.axis_index("tm").astype(jnp.int32)
    head = jnp.stack([jnp.int32(0), jnp.int32(0), jnp.int32(lax.axis_size("tm")), tm])
    bounds = jnp.concatenate([head, own]).astype(jnp.int32)
    g_conv, g_mix, g_down, g_bias = local_grads(
        bounds, x, xl, xr, te, tl, tr, wc, bc.reshape(1, C), wm, bm.reshape(1, C),
        wd, bd.reshape(1, CO))
    g_conv, g_mix, g_down, g_bias = lax.psum(
        (g_conv, g_mix, g_down, g_bias), ("tm", "weights", "batch"))
    scale = 1.0 / (jnp.sum(lengths).astype(jnp.float32) * CO)
    two = 2.0 * scale
    p, n = lax.axis_index("weights"), lax.axis_size("weights")

    def panel(a, dim):
        w = a.shape[dim] // n
        return lax.dynamic_slice_in_dim(a, p * w, w, dim) * two

    return (
        panel(g_conv, 2),
        panel(g_bias[2, C:], 0),
        panel(g_mix, 0),
        panel(g_bias[2, :C], 0),
        panel(g_down, 2),
        panel(g_bias[0], 0),
        (jnp.sum(g_bias[1]) * scale).reshape(1),
    )


def solution(mesh):
    clips = P(("groups", "weights", "batch"), "tm", None)
    return jax.shard_map(
        shards,
        mesh=mesh,
        in_specs=(clips, clips, P("groups"), P("groups")) + (P(),) * 6,
        out_specs=(
            P("groups", None, "weights"),
            P(("groups", "weights")),
            P(("groups", "weights"), None),
            P(("groups", "weights")),
            P("groups", None, "weights"),
            P(("groups", "weights")),
            P("groups"),
        ),
        check_vma=False,
    )
```

profile of v0, /device:TPU:0, one launch (start us, length us, event | category | flops | bytes accessed | tf_op | source)
XLA Modules:
  0.0 209.0 jit_solution(17682085893139780561)
XLA Ops:
  7.2 0.8 fusion.7
  8.0 4.9 %collective-permute-start = (f32[2,32,128]{2,1,0:T(8,128)S(1)}, f32[2,32,128]{2,1,0:T(8,128)S(1)}, u32[]{:S(2)}, u32[]{:S(2)}) collective-permute-start(f32[2,32,128]{2,1,0:T(8,128)S(1)} %get-tuple-element.28), channel_id=1, source_target_pairs={{0,4},{4,8},{8,12},{1,5},{5,9},{9,13},{2,6},{6,10},{10,14},{3,7},{... | collective-permute-start | bytes 98312 | tf_op jit(solution)/shard_map/ppermute | solution.py:224
  12.9 1.3 collective-permute-start.1
  14.2 0.7 fusion.6
  15.0 4.5 %collective-permute-start.2 = (f32[2,8,256]{2,1,0:T(8,128)S(1)}, f32[2,8,256]{2,1,0:T(8,128)S(1)}, u32[]{:S(2)}, u32[]{:S(2)}) collective-permute-start(f32[2,8,256]{2,1,0:T(8,128)S(1)} %get-tuple-element.26), channel_id=1, source_target_pairs={{0,4},{4,8},{8,12},{1,5},{5,9},{9,13},{2,6},{6,10},{10,14},{3,7},{... | collective-permute-start | bytes 49160 | tf_op jit(solution)/shard_map/ppermute | solution.py:224
  19.5 1.3 collective-permute-start.3
  20.8 0.8 dynamic-slice_bitcast_fusion
  21.8 1.3 reduce_sum.18
  23.8 1.3 collective-permute-done.3.tr
  25.2 1.6 copy-done
  26.7 1.0 copy-done.1
  27.8 1.0 copy-done.2
  28.8 0.8 copy-done.3
  29.6 0.7 copy-done.4
  30.3 0.7 copy-done.5
  31.0 0.7 copy-done.6
  31.6 40.2 %shard_map.153 = (f32[7,128,128]{2,1,0:T(8,128)}, f32[128,128]{1,0:T(8,128)}, f32[4,128,256]{2,1,0:T(8,128)}, f32[8,256]{1,0:T(8,128)S(1)}) custom-call(s32[8]{0:T(128)S(1)} %pad_add_fusion.1.bounds, f32[2,2048,128]{2,1,0:T(8,128)S(1)} %copy-done, f32[2,32,128]{2,1,0:T(8,128)S(1)} %collective-permute-done.xl, f32[2,32,128]{2,1,0:T(8,128)S(1)} %collective-permute-done.1.xr, ...), custom_call_target="tpu_custom_call" | custom-call | tf_op jit(solution)/shard_map/pallas_call | solution.py:192
  71.9 32.6 %psum.29 = f32[8,256]{1,0:T(8,128)S(1)} all-reduce(f32[8,256]{1,0:T(8,128)S(1)} %get-tuple-element.12), channel_id=1, replica_groups=mesh['groups'=2,'tm'=4,'weights'=2,'batch'=2] {'tm','weights','batch'}, use_global_device_ids=true, to_apply=%region_2.0 | all-reduce | flops 2048 | bytes 16384 | tf_op jit(solution)/shard_map/psum | solution.py:243
  104.5 0.6 slice_reduce_fusion
  107.5 89.2 %all-reduce.3.cloned.1.call-done = (f32[7,128,128]{2,1,0:T(8,128)}, f32[128,128]{1,0:T(8,128)}, f32[4,128,256]{2,1,0:T(8,128)}) async-done(((f32[7,128,128]{2,1,0:T(8,128)}, f32[128,128]{1,0:T(8,128)}, f32[4,128,256]{2,1,0:T(8,128)}), (f32[7,128,128]{2,1,0:T(8,128)}, f32[128,128]{1,0:T(8,128)}, f32[4,128,256]{2,1,0:T(8,128)})) %all-reduce.3.cloned.1.call-update) | async-done | bytes 1048592 | tf_op jit(solution)/shard_map/psum | solution.py:243
  196.7 1.2 dynamic-slice_multiply_fusion
  197.9 0.9 copy.18
  198.8 1.7 dynamic-slice_multiply_fusion.1
  200.4 0.6 dynamic-slice_multiply_fusion.2
  (23 shorter events, 2.0 us)
Async XLA Ops:
  7.2 189.5 %all-reduce.3.cloned.1.call-start = ((), (), s32[]{:S(2)}) async-start(), calls=%async_computation | async-start | bytes 2097152 | tf_op jit(solution)/shard_map/psum | solution.py:243
  8.0 17.1 %collective-permute-start = (f32[2,32,128]{2,1,0:T(8,128)S(1)}, f32[2,32,128]{2,1,0:T(8,128)S(1)}, u32[]{:S(2)}, u32[]{:S(2)}) collective-permute-start(f32[2,32,128]{2,1,0:T(8,128)S(1)} %get-tuple-element.28), channel_id=1, source_target_pairs={{0,4},{4,8},{8,12},{1,5},{5,9},{9,13},{2,6},{6,10},{10,14},{3,7},{... | collective-permute-start | bytes 98312 | tf_op jit(solution)/shard_map/ppermute | solution.py:224
  12.9 12.2 %collective-permute-start.1 = (f32[2,32,128]{2,1,0:T(8,128)S(1)}, f32[2,32,128]{2,1,0:T(8,128)S(1)}, u32[]{:S(2)}, u32[]{:S(2)}) collective-permute-start(f32[2,32,128]{2,1,0:T(8,128)S(1)} %get-tuple-element.27), channel_id=1, source_target_pairs={{4,0},{8,4},{12,8},{5,1},{9,5},{13,9},{6,2},{10,6},{14,10},{7,3},{... | collective-permute-start | bytes 98312 | tf_op jit(solution)/shard_map/ppermute | solution.py:224
  15.0 8.9 %collective-permute-start.2 = (f32[2,8,256]{2,1,0:T(8,128)S(1)}, f32[2,8,256]{2,1,0:T(8,128)S(1)}, u32[]{:S(2)}, u32[]{:S(2)}) collective-permute-start(f32[2,8,256]{2,1,0:T(8,128)S(1)} %get-tuple-element.26), channel_id=1, source_target_pairs={{0,4},{4,8},{8,12},{1,5},{5,9},{9,13},{2,6},{6,10},{10,14},{3,7},{... | collective-permute-start | bytes 49160 | tf_op jit(solution)/shard_map/ppermute | solution.py:224
  19.5 5.6 %collective-permute-start.3 = (f32[2,8,256]{2,1,0:T(8,128)S(1)}, f32[2,8,256]{2,1,0:T(8,128)S(1)}, u32[]{:S(2)}, u32[]{:S(2)}) collective-permute-start(f32[2,8,256]{2,1,0:T(8,128)S(1)} %get-tuple-element.25), channel_id=1, source_target_pairs={{4,0},{8,4},{12,8},{5,1},{9,5},{13,9},{6,2},{10,6},{14,10},{7,3},{... | collective-permute-start | bytes 49160 | tf_op jit(solution)/shard_map/ppermute | solution.py:224
  25.1 1.6 copy-start
  26.7 1.0 copy-start.1
  27.8 1.0 copy-start.2
  28.8 0.8 copy-start.3
  29.6 0.7 copy-start.4
  30.3 0.7 copy-start.5
  31.0 0.7 copy-start.6
  196.7 3.8 %copy-start.7 = (f32[128,128]{1,0:T(8,128)S(1)}, f32[128,128]{1,0:T(8,128)}, u32[]{:S(2)}) copy-start(f32[128,128]{1,0:T(8,128)} %get-tuple-element.23) | copy-start | bytes 196612
Sparse Core Ops, SparseCore 0:
  105.9 90.7 all-reduce.2
where the time goes:
time: 210 us; the launch traced here: 209 us
  waiting for transfers between devices  90.5 us (43%)
  Pallas kernels  40.2 us (19%)
  blocking collectives  32.6 us (16%)
  between operations  16.6 us (8%)
  starting transfers between devices  12.1 us (6%)
  local copies, waits for them, and re-layouts  9.82 us (5%)
  other arithmetic  7.19 us (3%)
    psum x1, waiting for transfers between devices, shards(): lax.psum((g_conv, g_mix, g_down, g_bias), ('tm', 'weights', 'batch'))  89.2 us
    pallas_call x1, Pallas kernels, local_grads(): pl.pallas_call(local_kernel, out_shape=outs, grid_spec=pltpu.PrefetchScal...  40.2 us
    psum x1, blocking collectives, shards(): lax.psum((g_conv, g_mix, g_down, g_bias), ('tm', 'weights', 'batch'))  32.6 us
    ppermute x4, starting transfers between devices, shift(): return lax.ppermute(a, 'tm', pairs)  12 us
    unnamed x17, local copies, waits for them, and re-layouts  7.35 us
    mul x6, other arithmetic, panel(): return lax.dynamic_slice_in_dim(a, p * w, w, dim) * two  5.21 us
  transfers between devices with their start and end apart: 5, of which 2 were waited for; matrix products, arithmetic and copies ran while one was open for 2% of the time, Pallas kernels for 0%

commit v1 on v0

--- a/solution.py
+++ b/solution.py
@@ -35,8 +35,8 @@
 
 def local_kernel(
     bounds, x, xl, xr, te, tl, tr, wc, bc, wm, bm, wd, bd,
-    o_conv, o_mix, o_down, o_bias,
-    act, ya, yb, hid, sec, d0, d1, dsec, dhid, w2, wb, acc2, accd,
+    o_all,
+    o_mix, o_bias, act, ya, yb, hid, sec, d0, d1, dsec, dhid, w2, wb, acc2, accd,
 ):
     step = pl.program_id(0)
     steps = pl.num_programs(0)
@@ -169,14 +169,23 @@
 
     @pl.when(step == steps - 1)
     def _():
-        for k in range(TAPS):
-            m, p = k // 2, k % 2
-            o_conv[k] = acc2[m * C:(m + 1) * C, p * C:(p + 1) * C]
-        for k in range(4):
-            o_down[k] = accd[k * C:(k + 1) * C]
-
-
-def local_grads(bounds, x, xl, xr, te, tl, tr, wc, bc, wm, bm, wd, bd):
+        h = C // 2
+        for p in range(2):
+            c = slice(p * h, (p + 1) * h)
+            d = slice(C + p * h, C + (p + 1) * h)
+            o_all[p, 0:4 * C, :h] = acc2[:, c]
+            o_all[p, 0:3 * C, h:] = acc2[0:3 * C, d]
+            o_all[p, 3 * C:3 * C + h, h:] = o_mix[c, :h]
+            o_all[p, 3 * C + h:4 * C, h:] = o_mix[c, h:]
+            o_all[p, 4 * C:8 * C] = accd[:, p * C:(p + 1) * C]
+            o_all[p, 8 * C:] = jnp.zeros_like(o_all[p, 8 * C:])
+            o_all[p, 8 * C:8 * C + 1] = o_bias[0:1, p * C:(p + 1) * C]
+            o_all[p, 8 * C + 1:8 * C + 2, :h] = o_bias[2:3, c]
+            o_all[p, 8 * C + 1:8 * C + 2, h:] = o_bias[2:3, d]
+            o_all[p, 8 * C + 2:8 * C + 3] = o_bias[1:2, :C] + o_bias[1:2, C:]
+
+
+def local_grads(rows, bounds, x, xl, xr, te, tl, tr, wc, bc, wm, bm, wd, bd):
     B, T, C = x.shape
     N, CO = te.shape[1:]
     f32 = jnp.float32
@@ -187,18 +196,19 @@
     def whole(a):
         return pl.BlockSpec(a.shape, lambda i, *_: (0,) * len(a.shape))
 
-    outs = [jax.ShapeDtypeStruct(s, f32) for s in
-            (wc.shape, wm.shape, wd.shape, (8, CO))]
+    out = jax.ShapeDtypeStruct((2, rows, C), f32)
     return pl.pallas_call(
         local_kernel,
-        out_shape=outs,
+        out_shape=out,
         grid_spec=pltpu.PrefetchScalarGridSpec(
             num_scalar_prefetch=1,
             grid=(B,),
             in_specs=[clip(a) for a in (x, xl, xr, te, tl, tr)]
             + [whole(a) for a in (wc, bc, wm, bm, wd, bd)],
-            out_specs=[whole(o) for o in outs],
+            out_specs=whole(out),
             scratch_shapes=[
+                pltpu.VMEM((C, C), f32),
+                pltpu.VMEM((8, CO), f32),
                 pltpu.VMEM((LEAD + T + HALO + 56, C), f32),
                 pltpu.VMEM((T + 32, C), f32),
                 pltpu.VMEM((T + 32, C), f32),
@@ -218,46 +228,216 @@
     )(bounds, x, xl, xr, te, tl, tr, wc, bc, wm, bm, wd, bd)
 
 
-def shift(a, up):
+def halo_kernel(x, te, xl, xr, tl, tr, sxl, sxr, stl, str_, send, recv):
     count = lax.axis_size("tm")
-    pairs = [(i, i + 1) if up else (i + 1, i) for i in range(count - 1)]
-    return lax.ppermute(a, "tm", pairs)
+    tm = lax.axis_index("tm")
+    T, N = x.shape[1], te.shape[1]
+    has_left, has_right = tm > 0, tm < count - 1
+    barrier = pltpu.get_barrier_semaphore()
+
+    def copy(k, src, dst, to):
+        return pltpu.make_async_remote_copy(
+            src_ref=src, dst_ref=dst, send_sem=send.at[k], recv_sem=recv.at[k],
+            device_id={"tm": to}, device_id_type=pl.DeviceIdType.MESH)
+
+    up = [copy(0, x.at[:, pl.ds(T - HALO, HALO)], sxl, tm + 1),
+          copy(1, te.at[:, pl.ds(N - 8, 8)], stl, tm + 1)]
+    down = [copy(2, x.at[:, pl.ds(0, HALO)], sxr, tm - 1),
+            copy(3, te.at[:, pl.ds(0, 8)], str_, tm - 1)]
+
+    @pl.when(has_left)
+    def _():
+        pl.semaphore_signal(barrier, inc=1, device_id={"tm": tm - 1},
+                            device_id_type=pl.DeviceIdType.MESH)
+
+    @pl.when(has_right)
+    def _():
+        pl.semaphore_signal(barrier, inc=1, device_id={"tm": tm + 1},
+                            device_id_type=pl.DeviceIdType.MESH)
+
+    pl.semaphore_wait(barrier, has_left.astype(jnp.int32) + has_right.astype(jnp.int32))
+
+    @pl.when(has_right)
+    def _():
+        for c in up:
+            c.start()
+
+    @pl.when(has_left)
+    def _():
+        for c in down:
+            c.start()
+
+    @pl.when(has_left)
+    def _():
+        for c in up:
+            c.wait_recv()
+        xl[...] = sxl[...]
+        tl[...] = stl[...]
+
+    @pl.when(tm == 0)
+    def _():
+        xl[...] = jnp.zeros_like(xl)
+        tl[...] = jnp.zeros_like(tl)
+
+    @pl.when(has_right)
+    def _():
+        for c in down:
+            c.wait_recv()
+        xr[...] = sxr[...]
+        tr[...] = str_[...]
+
+    @pl.when(tm == count - 1)
+    def _():
+        xr[...] = jnp.zeros_like(xr)
+        tr[...] = jnp.zeros_like(tr)
+
+    @pl.when(has_right)
+    def _():
+        for c in up:
+            c.wait_send()
+
+    @pl.when(has_left)
+    def _():
+        for c in down:
+            c.wait_send()
+
+
+def halos(x, te):
+    B, T, C = x.shape
+    CO = te.shape[2]
+    shapes = [(B, HALO, C), (B, HALO, C), (B, 8, CO), (B, 8, CO)]
+    return pl.pallas_call(
+        halo_kernel,
+        out_shape=[jax.ShapeDtypeStruct(s, jnp.float32) for s in shapes],
+        in_specs=[pl.BlockSpec(memory_space=pl.ANY)] * 2,
+        out_specs=[pl.BlockSpec(memory_space=pltpu.VMEM)] * 4,
+        scratch_shapes=[pltpu.VMEM(s, jnp.float32) for s in shapes]
+        + [pltpu.SemaphoreType.DMA((4,)), pltpu.SemaphoreType.DMA((4,))],
+        compiler_params=pltpu.CompilerParams(
+            collective_id=0, has_side_effects=True, vmem_limit_bytes=16 * 2**20),
+    )(x, te)
+
+
+def reduce_kernel(parts, full, near, total, slots, sem, send, recv, send2, recv2):
+    p = lax.axis_index("weights")
+    nb, n = lax.axis_size("batch"), lax.axis_size("batch") * lax.axis_size("tm")
+    me = lax.axis_index("tm") * nb + lax.axis_index("batch")
+    chunk = full.shape[0] // n
+
+    def place(d):
+        r = lax.rem(me + d, n)
+        return r, {"tm": r // nb, "batch": lax.rem(r, nb)}
+
+    barrier = pltpu.get_barrier_semaphore()
+    pl.semaphore_signal(barrier, inc=1, device_id={"weights": 1 - p},
+                        device_id_type=pl.DeviceIdType.MESH)
+
+    @pl.loop(1, n)
+    def _(d):
+        pl.semaphore_signal(barrier, inc=1, device_id=place(d)[1],
+                            device_id_type=pl.DeviceIdType.MESH)
+
+    pl.semaphore_wait(barrier, n)
+
+    swap = pltpu.make_async_remote_copy(
+        src_ref=parts.at[1 - p], dst_ref=near, send_sem=sem.at[0], recv_sem=sem.at[1],
+        device_id={"weights": 1 - p}, device_id_type=pl.DeviceIdType.MESH)
+    swap.start()
+    swap.wait()
+    total[...] = parts[p] + near[...]
+
+    def scatter(d):
+        r, to = place(d)
+        return pltpu.make_async_remote_copy(
+            src_ref=total.at[pl.ds(pl.multiple_of(r * chunk, 8), chunk)],
+            dst_ref=slots.at[d - 1], send_sem=send.at[d - 1], recv_sem=recv.at[d - 1],
+            device_id=to, device_id_type=pl.DeviceIdType.MESH)
+
+    @pl.loop(1, n)
+    def _(d):
+        scatter(d).start()
+
+    own = pl.ds(pl.multiple_of(me * chunk, 8), chunk)
+    full[own] = total[own]
+
+    @pl.loop(1, n)
+    def _(d):
+        scatter(d).wait_recv()
+        full[own] += slots[d - 1]
+
+    def gather(d, row):
+        return pltpu.make_async_remote_copy(
+            src_ref=full.at[own],
+            dst_ref=full.at[pl.ds(pl.multiple_of(row * chunk, 8), chunk)],
+            send_sem=send2.at[d - 1], recv_sem=recv2.at[d - 1],
+            device_id=place(d)[1], device_id_type=pl.DeviceIdType.MESH)
+
+    @pl.loop(1, n)
+    def _(d):
+        gather(d, me).start()
+
+    @pl.loop(1, n)
+    def _(d):
+        gather(d, lax.rem(me + n - d, n)).wait_recv()
+
+    @pl.loop(1, n)
+    def _(d):
+        scatter(d).wait_send()
+        gather(d, me).wait_send()
+
+
+def total_panel(parts):
+    rows, C = parts.shape[1:]
+    n = lax.axis_size("batch") * lax.axis_size("tm")
+    f32 = jnp.float32
+    dma = pltpu.SemaphoreType.DMA
+    return pl.pallas_call(
+        reduce_kernel,
+        out_shape=jax.ShapeDtypeStruct((rows, C), f32),
+        in_specs=[pl.BlockSpec(memory_space=pltpu.VMEM)],
+        out_specs=pl.BlockSpec(memory_space=pltpu.VMEM),
+        scratch_shapes=[
+            pltpu.VMEM((rows, C), f32),
+            pltpu.VMEM((rows, C), f32),
+            pltpu.VMEM((n - 1, rows // n, C), f32),
+            dma((2,)), dma((n - 1,)), dma((n - 1,)), dma((n - 1,)), dma((n - 1,)),
+        ],
+        compiler_params=pltpu.CompilerParams(
+            collective_id=1, has_side_effects=True, vmem_limit_bytes=24 * 2**20),
+    )(parts)
 
 
 def shards(x, te, starts, lengths, wc, bc, wm, bm, wd, bd):
     B, T, C = x.shape
     N, CO = te.shape[1:]
-    xl = shift(x[:, T - HALO:], True)
-    xr = shift(x[:, :HALO], False)
-    tl = shift(te[:, N - 8:], True)
-    tr = shift(te[:, :8], False)
+    xl, xr, tl, tr = halos(x, te)
     mine = lax.axis_index(("weights", "batch")) * B
     own = jnp.stack([lax.dynamic_slice_in_dim(starts, mine, B),
                      lax.dynamic_slice_in_dim(lengths, mine, B)], axis=1).reshape(-1)
     tm = lax.axis_index("tm").astype(jnp.int32)
     head = jnp.stack([jnp.int32(0), jnp.int32(0), jnp.int32(lax.axis_size("tm")), tm])
     bounds = jnp.concatenate([head, own]).astype(jnp.int32)
-    g_conv, g_mix, g_down, g_bias = local_grads(
-        bounds, x, xl, xr, te, tl, tr, wc, bc.reshape(1, C), wm, bm.reshape(1, C),
+    n = lax.axis_size("batch") * lax.axis_size("tm")
+    rows = -(-(8 * C + 8) // (8 * n)) * 8 * n
+    parts = local_grads(
+        rows, bounds, x, xl, xr, te, tl, tr, wc, bc.reshape(1, C), wm, bm.reshape(1, C),
         wd, bd.reshape(1, CO))
-    g_conv, g_mix, g_down, g_bias = lax.psum(
-        (g_conv, g_mix, g_down, g_bias), ("tm", "weights", "batch"))
     scale = 1.0 / (jnp.sum(lengths).astype(jnp.float32) * CO)
-    two = 2.0 * scale
-    p, n = lax.axis_index("weights"), lax.axis_size("weights")
-
-    def panel(a, dim):
-        w = a.shape[dim] // n
-        return lax.dynamic_slice_in_dim(a, p * w, w, dim) * two
-
+    g = total_panel(parts)
+    s = g * (2.0 * scale)
+    h = C // 2
+    low = s[:4 * C, :h].reshape(4, C, h)
+    high = s[:3 * C, h:].reshape(3, C, h)
+    g_conv = jnp.stack([low[0], high[0], low[1], high[1], low[2], high[2], low[3]])
+    g_mix = jnp.concatenate([s[3 * C:3 * C + h, h:], s[3 * C + h:4 * C, h:]], axis=1)
     return (
-        panel(g_conv, 2),
-        panel(g_bias[2, C:], 0),
-        panel(g_mix, 0),
-        panel(g_bias[2, :C], 0),
-        panel(g_down, 2),
-        panel(g_bias[0], 0),
-        (jnp.sum(g_bias[1]) * scale).reshape(1),
+        g_conv,
+        s[8 * C + 1, h:],
+        g_mix,
+        s[8 * C + 1, :h],
+        s[4 * C:8 * C].reshape(4, C, C),
+        s[8 * C],
+        (jnp.sum(g[8 * C + 2]) * scale).reshape(1),
     )
 
 

time: 210 us -> 89.8 us (0.43)
  the two profiles are of different devices: /device:TPU:0 before, /device:TPU:29 now
where the time goes in v1:
time: 89.8 us; the launch traced here: 88.5 us
  Pallas kernels  75.3 us (84%)
  local copies, waits for them, and re-layouts  7.18 us (8%)
  between operations  3.27 us (4%)
  other arithmetic  2.73 us (3%)
    pallas_call x1, Pallas kernels, local_grads(): pl.pallas_call(local_kernel, out_shape=out, grid_spec=pltpu.PrefetchScala...  39.7 us
    pallas_call x1, Pallas kernels, total_panel(): pl.pallas_call(reduce_kernel, out_shape=jax.ShapeDtypeStruct((rows, C), f...  32.6 us
    unnamed x25, local copies, waits for them, and re-layouts  4.34 us
    pallas_call x1, Pallas kernels, halos(): pl.pallas_call(halo_kernel, out_shape=[jax.ShapeDtypeStruct(s, jnp.float3...  3.06 us

profile of v1, /device:TPU:29, one launch (start us, length us, event | category | flops | bytes accessed | tf_op | source)
XLA Modules:
  0.0 88.5 jit_solution(5069406425621122274)
XLA Ops:
  0.6 1.3 %reduce_sum.18 = s32[]{:T(128)} reduce(s32[8]{0:T(128)} %param.13, s32[]{:T(128)} %constant.11.clone.1), dimensions={0}, to_apply=%region_0.0 | reduce | flops 7 | bytes 40 | tf_op jit(solution)/shard_map/reduce_sum | solution.py:425
  2.6 0.8 dynamic-slice_bitcast_fusion
  3.4 0.1 copy.17
  3.5 0.1 reshape.41
  3.6 0.1 pad_add_fusion.1.bounds
  3.7 1.6 %copy-done = f32[2,2048,128]{2,1,0:T(8,128)S(1)} copy-done((f32[2,2048,128]{2,1,0:T(8,128)S(1)}, f32[2,2048,128]{2,1,0:T(8,128)}, u32[]{:S(2)}) %copy-start) | copy-done | bytes 2097176
  5.2 1.6 %copy-done.2 = f32[2,1024,256]{2,1,0:T(8,128)S(1)} copy-done((f32[2,1024,256]{2,1,0:T(8,128)S(1)}, f32[2,1024,256]{2,1,0:T(8,128)}, u32[]{:S(2)}) %copy-start.2) | copy-done | bytes 2097176
  6.9 0.0 copy-start.6
  6.9 0.0 copy-start.7
  6.9 0.0 copy-start.8
  6.9 3.1 %shard_map.153 = (f32[2,32,128]{2,1,0:T(8,128)S(1)}, f32[2,32,128]{2,1,0:T(8,128)S(1)}, f32[2,8,256]{2,1,0:T(8,128)S(1)}, f32[2,8,256]{2,1,0:T(8,128)S(1)}) custom-call(f32[2,2048,128]{2,1,0:T(8,128)S(1)} %copy-done, f32[2,1024,256]{2,1,0:T(8,128)S(1)} %copy-done.2), custom_call_target="tpu_custom_call" | custom-call | tf_op jit(solution)/shard_map/pallas_call | solution.py:309
  10.0 0.0 copy-done.1
  10.0 39.7 %shard_map.154.parts = f32[2,1088,128]{2,1,0:T(8,128)S(1)} custom-call(s32[8]{0:T(128)S(1)} %pad_add_fusion.1.bounds, f32[2,2048,128]{2,1,0:T(8,128)S(1)} %copy-done.1, f32[2,32,128]{2,1,0:T(8,128)S(1)} %get-tuple-element.11.xl, f32[2,32,128]{2,1,0:T(8,128)S(1)} %get-tuple-element.12.xr, f32[2,1024,256]{2,1,0:T(8,128)} %te.3, ...), custom_call_target="tpu_custom_call" | custom-call | tf_op jit(solution)/shard_map/pallas_call | solution.py:200
  49.7 32.6 %shard_map.155 = f32[1088,128]{1,0:T(8,128)S(1)} custom-call(f32[2,1088,128]{2,1,0:T(8,128)S(1)} %shard_map.154.parts), custom_call_target="tpu_custom_call" | custom-call | tf_op jit(solution)/shard_map/pallas_call | solution.py:394
  82.3 0.6 slice_reduce_fusion
  83.6 0.5 slice_bitcast_fusion.7
  84.1 0.6 slice_bitcast_fusion.8
  84.7 0.1 fusion.7
  84.8 0.7 pad_maximum_fusion
  85.5 0.7 slice.104
  86.2 0.1 fusion.5
  86.3 0.1 fusion.3
  86.4 0.1 fusion.1
  86.5 0.9 copy.18
  (19 shorter events, 0.1 us)
Async XLA Ops:
  3.7 1.6 %copy-start = (f32[2,2048,128]{2,1,0:T(8,128)S(1)}, f32[2,2048,128]{2,1,0:T(8,128)}, u32[]{:S(2)}) copy-start(f32[2,2048,128]{2,1,0:T(8,128)} %x.3) | copy-start | bytes 6291460
  5.2 1.6 %copy-start.2 = (f32[2,1024,256]{2,1,0:T(8,128)S(1)}, f32[2,1024,256]{2,1,0:T(8,128)}, u32[]{:S(2)}) copy-start(f32[2,1024,256]{2,1,0:T(8,128)} %te.3) | copy-start | bytes 6291460
  6.8 3.1 %copy-start.1 = (f32[2,2048,128]{2,1,0:T(8,128)S(1)}, f32[2,2048,128]{2,1,0:T(8,128)}, u32[]{:S(2)}) copy-start(f32[2,2048,128]{2,1,0:T(8,128)} %x.3) | copy-start | bytes 6291460
  6.8 3.1 %copy-start.3 = (f32[4,128,256]{2,1,0:T(8,128)S(1)}, f32[4,128,256]{2,1,0:T(8,128)}, u32[]{:S(2)}) copy-start(f32[4,128,256]{2,1,0:T(8,128)} %wd.1) | copy-start | bytes 1572868
  6.8 3.1 %copy-start.4 = (f32[7,128,128]{2,1,0:T(8,128)S(1)}, f32[7,128,128]{2,1,0:T(8,128)}, u32[]{:S(2)}) copy-start(f32[7,128,128]{2,1,0:T(8,128)} %wc.1) | copy-start | bytes 1376260
  6.8 3.1 %copy-start.5 = (f32[128,128]{1,0:T(8,128)S(1)}, f32[128,128]{1,0:T(8,128)}, u32[]{:S(2)}) copy-start(f32[128,128]{1,0:T(8,128)} %wm.1) | copy-start | bytes 196612
  6.9 3.2 %copy-start.6 = (f32[256]{0:T(256)S(1)}, f32[256]{0:T(256)}, u32[]{:S(2)}) copy-start(f32[256]{0:T(256)} %param.19) | copy-start | bytes 3076
  6.9 3.1 %copy-start.7 = (f32[128]{0:T(128)S(1)}, f32[128]{0:T(128)}, u32[]{:S(2)}) copy-start(f32[128]{0:T(128)} %param.15) | copy-start | bytes 1540
  6.9 3.1 %copy-start.8 = (f32[128]{0:T(128)S(1)}, f32[128]{0:T(128)}, u32[]{:S(2)}) copy-start(f32[128]{0:T(128)} %param.17) | copy-start | bytes 1540

commit v2 on v1

--- a/solution.py
+++ b/solution.py
@@ -23,40 +23,59 @@
     return jnp.where(e > 0, 1.0, e + 1.0)
 
 
-def mm(a, b):
-    return lax.dot_general(a, b, (((1,), (0,)), ((), ())), precision=lax.Precision.HIGH,
-                           preferred_element_type=jnp.float32)
+def split(a):
+    hi = a.astype(jnp.bfloat16)
+    return hi, (a - hi.astype(jnp.float32)).astype(jnp.bfloat16)
+
+
+def three(a, b, dims):
+    def dot(u, v):
+        return lax.dot_general(u, v, (dims, ((), ())), preferred_element_type=jnp.float32)
+
+    return dot(a[0], b[0]) + dot(a[1], b[0]) + dot(a[0], b[1])
+
+
+def mm(a, w):
+    return three(split(a), (w[0], w[1]), ((1,), (0,)))
 
 
 def mm_t(a, b):
-    return lax.dot_general(a, b, (((0,), (0,)), ((), ())), precision=lax.Precision.HIGH,
-                           preferred_element_type=jnp.float32)
+    return three(split(a), split(b), ((0,), (0,)))
 
 
 def local_kernel(
-    bounds, x, xl, xr, te, tl, tr, wc, bc, wm, bm, wd, bd,
+    starts, lengths, x, xl, xr, te, tl, tr, wc, bc, wm, bm, wd, bd,
     o_all,
-    o_mix, o_bias, act, ya, yb, hid, sec, d0, d1, dsec, dhid, w2, wb, acc2, accd,
+    o_mix, o_bias, act, ya, yb, hid, sec, d0, d1, dsec, dhid, w2, wb, wf, wx, acc2, accd,
 ):
     step = pl.program_id(0)
     steps = pl.num_programs(0)
     T, C = x.shape[1], x.shape[2]
     N, CO = te.shape[1], te.shape[2]
-    t0 = bounds[3] * T
-    j0 = bounds[3] * N
-    total = bounds[2] * T
-    first = bounds[4 + 2 * step]
-    last = first + bounds[5 + 2 * step]
+    tm = lax.axis_index("tm")
+    t0, j0 = tm * T, tm * N
+    total = lax.axis_size("tm") * T
+    clip = lax.axis_index(("weights", "batch")) * steps + step
+    first = starts[clip]
+    last = first + lengths[clip]
 
     @pl.when(step == 0)
     def _():
+        def put(w, rows, cols, value):
+            hi, lo = split(value)
+            w[0, rows, cols] = hi
+            w[1, rows, cols] = lo
+
         for k in range(TAPS + 1):
             m, p = k // 2, k % 2
-            w2[m * C:(m + 1) * C, p * C:(p + 1) * C] = (
+            put(w2, slice(m * C, (m + 1) * C), slice(p * C, (p + 1) * C),
                 wc[k] if k < TAPS else jnp.zeros((C, C), jnp.float32))
         for k in range(4):
             r, p = k // 2, k % 2
-            wb[r * CO:(r + 1) * CO, p * C:(p + 1) * C] = wd[k].T
+            put(wb, slice(r * CO, (r + 1) * CO), slice(p * C, (p + 1) * C), wd[k].T)
+            put(wf, slice(k * C, (k + 1) * C), slice(0, CO), wd[k])
+        put(wx, slice(0, C), slice(0, C), wm[...])
+        put(wx, slice(C, 2 * C), slice(0, C), wm[...].T)
         acc2[...] = jnp.zeros_like(acc2)
         accd[...] = jnp.zeros_like(accd)
         o_mix[...] = jnp.zeros_like(o_mix)
@@ -78,7 +97,7 @@
     def conv(t, n):
         a = jnp.concatenate(
             [act[pl.ds(LEAD - 27 + 18 * m + t, n)] for m in range(4)], axis=1)
-        r = mm(a, w2[...])
+        r = mm(a, w2)
         row = pl.ds(8 + t, n)
         ya[row] = r[:, :C]
         yb[row] = r[:, C:]
@@ -93,7 +112,7 @@
         h = ya[pl.ds(8 + t, n)] + yb[pl.ds(17 + t, n)] + bc[...]
         g = elu(h)
         hid[pl.ds(8 + t, n)] = g
-        v = elu(xv + mm(g, wm[...]) + bm[...])
+        v = elu(xv + mm(g, (wx[0, :C], wx[1, :C])) + bm[...])
         pos = t0 + t + lax.broadcasted_iota(jnp.int32, (n, C), 0)
         sec[pl.ds(EDGE + t, n)] = jnp.where((pos >= 0) & (pos < total), v, 0.0)
 
@@ -108,7 +127,7 @@
     def error(j, n, tv):
         a = jnp.concatenate(
             [sec[pl.ds(EDGE + 2 * j + k - 1, n, stride=2)] for k in range(4)], axis=1)
-        e = mm(a, wd[...].reshape(4 * C, CO)) + bd[...] - tv
+        e = mm(a, wf) + bd[...] - tv
         pos = j0 + j + lax.broadcasted_iota(jnp.int32, (n, CO), 0)
         d = jnp.where((pos >= first) & (pos < last), e, 0.0)
         d0[pl.ds(8 + j, n)] = d[:, :C]
@@ -130,7 +149,7 @@
         b = jnp.concatenate(
             [d0[pl.ds(8 + j, n)], d1[pl.ds(8 + j, n)],
              d0[pl.ds(7 + j, n)], d1[pl.ds(7 + j, n)]], axis=1)
-        r = mm(b, wb[...])
+        r = mm(b, wb)
         dsec[pl.ds(EDGE + 2 * j - 1, n, stride=2)] = r[:, :C]
         dsec[pl.ds(EDGE + 2 * j, n, stride=2)] = r[:, C:]
 
@@ -146,9 +165,7 @@
         ds = dsec[pl.ds(EDGE + s, CHUNK)] * slope(sec[pl.ds(EDGE + s, CHUNK)])
         g = hid[pl.ds(8 + s, CHUNK)]
         o_mix[...] += mm_t(g, ds)
-        dg = lax.dot_general(ds, wm[...], (((1,), (1,)), ((), ())),
-                             precision=lax.Precision.HIGH,
-                             preferred_element_type=jnp.float32)
+        dg = mm(ds, (wx[0, C:], wx[1, C:]))
         dh = dg * slope(g)
         dhid[pl.ds(16 + s, CHUNK)] = dh
         o_bias[2:3, :C] += jnp.sum(ds, axis=0, keepdims=True)
@@ -170,22 +187,26 @@
     @pl.when(step == steps - 1)
     def _():
         h = C // 2
+        count = lax.fori_loop(
+            0, lengths.shape[0], lambda i, c: c + lengths[i], jnp.int32(0))
+        scale = 1.0 / (jnp.full((1, C), count.astype(jnp.float32)) * CO)
+        two = 2.0 * scale
         for p in range(2):
             c = slice(p * h, (p + 1) * h)
             d = slice(C + p * h, C + (p + 1) * h)
-            o_all[p, 0:4 * C, :h] = acc2[:, c]
-            o_all[p, 0:3 * C, h:] = acc2[0:3 * C, d]
-            o_all[p, 3 * C:3 * C + h, h:] = o_mix[c, :h]
-            o_all[p, 3 * C + h:4 * C, h:] = o_mix[c, h:]
-            o_all[p, 4 * C:8 * C] = accd[:, p * C:(p + 1) * C]
+            o_all[p, 0:4 * C, :h] = acc2[:, c] * two[:, :h]
+            o_all[p, 0:3 * C, h:] = acc2[0:3 * C, d] * two[:, :h]
+            o_all[p, 3 * C:3 * C + h, h:] = o_mix[c, :h] * two[:, :h]
+            o_all[p, 3 * C + h:4 * C, h:] = o_mix[c, h:] * two[:, :h]
+            o_all[p, 4 * C:8 * C] = accd[:, p * C:(p + 1) * C] * two
             o_all[p, 8 * C:] = jnp.zeros_like(o_all[p, 8 * C:])
-            o_all[p, 8 * C:8 * C + 1] = o_bias[0:1, p * C:(p + 1) * C]
-            o_all[p, 8 * C + 1:8 * C + 2, :h] = o_bias[2:3, c]
-            o_all[p, 8 * C + 1:8 * C + 2, h:] = o_bias[2:3, d]
-            o_all[p, 8 * C + 2:8 * C + 3] = o_bias[1:2, :C] + o_bias[1:2, C:]
-
-
-def local_grads(rows, bounds, x, xl, xr, te, tl, tr, wc, bc, wm, bm, wd, bd):
+            o_all[p, 8 * C:8 * C + 1] = o_bias[0:1, p * C:(p + 1) * C] * two
+            o_all[p, 8 * C + 1:8 * C + 2, :h] = o_bias[2:3, c] * two[:, :h]
+            o_all[p, 8 * C + 2:8 * C + 3, :h] = o_bias[2:3, d] * two[:, :h]
+            o_all[p, 8 * C + 3:8 * C + 4] = (o_bias[1:2, :C] + o_bias[1:2, C:]) * scale
+
+
+def local_grads(rows, starts, lengths, x, xl, xr, te, tl, tr, wc, bc, wm, bm, wd, bd):
     B, T, C = x.shape
     N, CO = te.shape[1:]
     f32 = jnp.float32
@@ -201,7 +222,7 @@
         local_kernel,
         out_shape=out,
         grid_spec=pltpu.PrefetchScalarGridSpec(
-            num_scalar_prefetch=1,
+            num_scalar_prefetch=2,
             grid=(B,),
             in_specs=[clip(a) for a in (x, xl, xr, te, tl, tr)]
             + [whole(a) for a in (wc, bc, wm, bm, wd, bd)],
@@ -218,14 +239,16 @@
                 pltpu.VMEM((N + 16, CO // 2), f32),
                 pltpu.VMEM((EDGE + T + 32, C), f32),
                 pltpu.VMEM((T + 32, C), f32),
-                pltpu.VMEM((4 * C, 2 * C), f32),
-                pltpu.VMEM((2 * CO, 2 * C), f32),
+                pltpu.VMEM((2, 4 * C, 2 * C), jnp.bfloat16),
+                pltpu.VMEM((2, 2 * CO, 2 * C), jnp.bfloat16),
+                pltpu.VMEM((2, 4 * C, CO), jnp.bfloat16),
+                pltpu.VMEM((2, 2 * C, C), jnp.bfloat16),
                 pltpu.VMEM((4 * C, 2 * C), f32),
                 pltpu.VMEM((4 * C, CO), f32),
             ],
         ),
-        compiler_params=pltpu.CompilerParams(vmem_limit_bytes=48 * 2**20),
-    )(bounds, x, xl, xr, te, tl, tr, wc, bc, wm, bm, wd, bd)
+        compiler_params=pltpu.CompilerParams(vmem_limit_bytes=58 * 2**20),
+    )(starts, lengths, x, xl, xr, te, tl, tr, wc, bc, wm, bm, wd, bd)
 
 
 def halo_kernel(x, te, xl, xr, tl, tr, sxl, sxr, stl, str_, send, recv):
@@ -314,11 +337,11 @@
         scratch_shapes=[pltpu.VMEM(s, jnp.float32) for s in shapes]
         + [pltpu.SemaphoreType.DMA((4,)), pltpu.SemaphoreType.DMA((4,))],
         compiler_params=pltpu.CompilerParams(
-            collective_id=0, has_side_effects=True, vmem_limit_bytes=16 * 2**20),
+            collective_id=0, has_side_effects=True, vmem_limit_bytes=58 * 2**20),
     )(x, te)
 
 
-def reduce_kernel(parts, full, near, total, slots, sem, send, recv, send2, recv2):
+def reduce_kernel(parts, full, near, total, slots, ssend, srecv, send, recv, send2, recv2):
     p = lax.axis_index("weights")
     nb, n = lax.axis_size("batch"), lax.axis_size("batch") * lax.axis_size("tm")
     me = lax.axis_index("tm") * nb + lax.axis_index("batch")
@@ -339,12 +362,19 @@
 
     pl.semaphore_wait(barrier, n)
 
-    swap = pltpu.make_async_remote_copy(
-        src_ref=parts.at[1 - p], dst_ref=near, send_sem=sem.at[0], recv_sem=sem.at[1],
-        device_id={"weights": 1 - p}, device_id_type=pl.DeviceIdType.MESH)
-    swap.start()
-    swap.wait()
-    total[...] = parts[p] + near[...]
+    def rows(d):
+        r = lax.rem(me + d, n)
+        return pl.ds(pl.multiple_of(r * chunk, 8), chunk)
+
+    def swap(d):
+        return pltpu.make_async_remote_copy(
+            src_ref=parts.at[1 - p, rows(d)], dst_ref=near.at[rows(d)],
+            send_sem=ssend.at[d - 1], recv_sem=srecv.at[d - 1],
+            device_id={"weights": 1 - p}, device_id_type=pl.DeviceIdType.MESH)
+
+    @pl.loop(1, n + 1)
+    def _(d):
+        swap(d).start()
 
     def scatter(d):
         r, to = place(d)
@@ -355,10 +385,13 @@
 
     @pl.loop(1, n)
     def _(d):
+        swap(d).wait_recv()
+        total[rows(d)] = parts[p, rows(d)] + near[rows(d)]
         scatter(d).start()
 
     own = pl.ds(pl.multiple_of(me * chunk, 8), chunk)
-    full[own] = total[own]
+    swap(n).wait_recv()
+    full[own] = parts[p, own] + near[own]
 
     @pl.loop(1, n)
     def _(d):
@@ -384,6 +417,10 @@
     def _(d):
         scatter(d).wait_send()
         gather(d, me).wait_send()
+
+    @pl.loop(1, n + 1)
+    def _(d):
+        swap(d).wait_send()
 
 
 def total_panel(parts):
@@ -400,45 +437,54 @@
             pltpu.VMEM((rows, C), f32),
             pltpu.VMEM((rows, C), f32),
             pltpu.VMEM((n - 1, rows // n, C), f32),
-            dma((2,)), dma((n - 1,)), dma((n - 1,)), dma((n - 1,)), dma((n - 1,)),
+            dma((n,)), dma((n,)), dma((n - 1,)), dma((n - 1,)), dma((n - 1,)), dma((n - 1,)),
         ],
         compiler_params=pltpu.CompilerParams(
             collective_id=1, has_side_effects=True, vmem_limit_bytes=24 * 2**20),
     )(parts)
 
 
+def unpack_kernel(g, conv, conv_b, mix, mix_b, down, down_b, loss):
+    C = g.shape[1]
+    h = C // 2
+    for k in range(TAPS):
+        m = k // 2
+        conv[k] = g[m * C:(m + 1) * C, (k % 2) * h:(k % 2 + 1) * h]
+    mix[:, :h] = g[3 * C:3 * C + h, h:]
+    mix[:, h:] = g[3 * C + h:4 * C, h:]
+    for k in range(4):
+        down[k] = g[(4 + k) * C:(5 + k) * C]
+    down_b[...] = g[8 * C:8 * C + 1]
+    mix_b[...] = g[8 * C + 1:8 * C + 2, :h]
+    conv_b[...] = g[8 * C + 2:8 * C + 3, :h]
+    loss[...] = jnp.sum(g[8 * C + 3:8 * C + 4], axis=1, keepdims=True)
+
+
+def unpack(g):
+    C = g.shape[1]
+    h = C // 2
+    shapes = [(TAPS, C, h), (1, h), (h, C), (1, h), (4, C, C), (1, C), (1, 1)]
+    vmem = pl.BlockSpec(memory_space=pltpu.VMEM)
+    return pl.pallas_call(
+        unpack_kernel,
+        out_shape=[jax.ShapeDtypeStruct(s, jnp.float32) for s in shapes],
+        in_specs=[vmem],
+        out_specs=[vmem] * len(shapes),
+        compiler_params=pltpu.CompilerParams(vmem_limit_bytes=16 * 2**20),
+    )(g)
+
+
 def shards(x, te, starts, lengths, wc, bc, wm, bm, wd, bd):
-    B, T, C = x.shape
-    N, CO = te.shape[1:]
+    C, CO = x.shape[2], te.shape[2]
     xl, xr, tl, tr = halos(x, te)
-    mine = lax.axis_index(("weights", "batch")) * B
-    own = jnp.stack([lax.dynamic_slice_in_dim(starts, mine, B),
-                     lax.dynamic_slice_in_dim(lengths, mine, B)], axis=1).reshape(-1)
-    tm = lax.axis_index("tm").astype(jnp.int32)
-    head = jnp.stack([jnp.int32(0), jnp.int32(0), jnp.int32(lax.axis_size("tm")), tm])
-    bounds = jnp.concatenate([head, own]).astype(jnp.int32)
     n = lax.axis_size("batch") * lax.axis_size("tm")
     rows = -(-(8 * C + 8) // (8 * n)) * 8 * n
     parts = local_grads(
-        rows, bounds, x, xl, xr, te, tl, tr, wc, bc.reshape(1, C), wm, bm.reshape(1, C),
-        wd, bd.reshape(1, CO))
-    scale = 1.0 / (jnp.sum(lengths).astype(jnp.float32) * CO)
-    g = total_panel(parts)
-    s = g * (2.0 * scale)
-    h = C // 2
-    low = s[:4 * C, :h].reshape(4, C, h)
-    high = s[:3 * C, h:].reshape(3, C, h)
-    g_conv = jnp.stack([low[0], high[0], low[1], high[1], low[2], high[2], low[3]])
-    g_mix = jnp.concatenate([s[3 * C:3 * C + h, h:], s[3 * C + h:4 * C, h:]], axis=1)
-    return (
-        g_conv,
-        s[8 * C + 1, h:],
-        g_mix,
-        s[8 * C + 1, :h],
-        s[4 * C:8 * C].reshape(4, C, C),
-        s[8 * C],
-        (jnp.sum(g[8 * C + 2]) * scale).reshape(1),
-    )
+        rows, starts, lengths, x, xl, xr, te, tl, tr, wc, bc.reshape(1, C), wm,
+        bm.reshape(1, C), wd, bd.reshape(1, CO))
+    conv, conv_b, mix, mix_b, down, down_b, loss = unpack(total_panel(parts))
+    return (conv, conv_b.reshape(-1), mix, mix_b.reshape(-1), down,
+            down_b.reshape(-1), loss.reshape(1))
 
 
 def solution(mesh):

time: 89.8 us -> 81.5 us (0.908); the launches traced: 88.5 us -> 81.4 us
  local copies, waits for them, and re-layouts: 7.18 us -> 2.12 us
  Pallas kernels: 75.3 us -> 78.6 us
  other arithmetic: 2.73 us -> 0 us
  between operations: 3.27 us -> 0.65 us
    unnamed x25 -> x3, local copies, waits for them, and re-layouts: 4.34 us -> 2.12 us
    reduce_sum x2 -> x0, other arithmetic: 1.89 us -> none  [the longest x1 1.29 us: shards(): scale = 1.0 / (jnp.sum(lengths).astype(jnp.float32) * CO)]
    pallas_call x1, Pallas kernels: 39.7 us -> 41.4 us  [local_grads(): pl.pallas_call(local_kernel, out_shape=out, grid_spec=pltpu.PrefetchScala...]
    squeeze x2 -> x0, local copies, waits for them, and re-layouts: 1.09 us -> none  [the longest x1 0.58 us: shards(): s[8 * C + 1, :h]]
where the time goes in v2:
time: 81.5 us; the launch traced here: 81.4 us
  Pallas kernels  78.6 us (96%)
  local copies, waits for them, and re-layouts  2.12 us (3%)
    pallas_call x1, Pallas kernels, local_grads(): pl.pallas_call(local_kernel, out_shape=out, grid_spec=pltpu.PrefetchScala...  41.4 us
    pallas_call x1, Pallas kernels, total_panel(): pl.pallas_call(reduce_kernel, out_shape=jax.ShapeDtypeStruct((rows, C), f...  32.5 us
    pallas_call x1, Pallas kernels, halos(): pl.pallas_call(halo_kernel, out_shape=[jax.ShapeDtypeStruct(s, jnp.float3...  3.92 us
    unnamed x3, local copies, waits for them, and re-layouts  2.12 us

profile of v2, /device:TPU:29, one launch (start us, length us, event | category | flops | bytes accessed | tf_op | source)
XLA Modules:
  0.0 81.4 jit_solution(7201023198662472362)
XLA Ops:
  0.6 3.9 %shard_map.153 = (f32[2,32,128]{2,1,0:T(8,128)}, f32[2,32,128]{2,1,0:T(8,128)}, f32[2,8,256]{2,1,0:T(8,128)}, f32[2,8,256]{2,1,0:T(8,128)}) custom-call(f32[2,2048,128]{2,1,0:T(8,128)} %x.3, f32[2,1024,256]{2,1,0:T(8,128)} %te.3), custom_call_target="tpu_custom_call" | custom-call | tf_op jit(solution)/shard_map/pallas_call | solution.py:332
  4.6 41.4 %shard_map.154.parts = f32[2,1088,128]{2,1,0:T(8,128)} custom-call(s32[8]{0:T(128)} %starts.1, s32[8]{0:T(128)} %lengths.1, f32[2,2048,128]{2,1,0:T(8,128)} %x.3, f32[2,32,128]{2,1,0:T(8,128)} %get-tuple-element.18.xl, f32[2,32,128]{2,1,0:T(8,128)} %get-tuple-element.19.xr, f32[2,1024,256]{2,1,0:T(8,128)} %te.3, f32[2,8,256]{2,1,0:T(8,128)} %get-tuple-element.20.tl, ...), custom_call_target="tpu_custom_call" | custom-call | tf_op jit(solution)/shard_map/pallas_call | solution.py:221
  45.9 0.0 copy-start
  45.9 1.2 %copy-done = f32[2,1088,128]{2,1,0:T(8,128)S(1)} copy-done((f32[2,1088,128]{2,1,0:T(8,128)S(1)}, f32[2,1088,128]{2,1,0:T(8,128)}, u32[]{:S(2)}) %copy-start) | copy-done | bytes 1114136
  47.2 32.5 %shard_map.155.g = f32[1088,128]{1,0:T(8,128)S(1)} custom-call(f32[2,1088,128]{2,1,0:T(8,128)S(1)} %copy-done), custom_call_target="tpu_custom_call" | custom-call | tf_op jit(solution)/shard_map/pallas_call | solution.py:431
  79.7 0.8 shard_map.156
  80.5 0.9 %copy.17 = f32[7,128,64]{1,2,0:T(8,128)} copy(f32[7,128,64]{2,1,0:T(8,128)S(1)} %get-tuple-element.29) | data formatting | bytes 458752
Async XLA Ops:
  45.9 1.2 %copy-start = (f32[2,1088,128]{2,1,0:T(8,128)S(1)}, f32[2,1088,128]{2,1,0:T(8,128)}, u32[]{:S(2)}) copy-start(f32[2,1088,128]{2,1,0:T(8,128)} %shard_map.154.parts) | copy-start | bytes 3342340

commit v3 on v2

--- a/solution.py
+++ b/solution.py
@@ -12,7 +12,7 @@
 HALO = 32
 LEAD = 40
 EDGE = 24
-CHUNK = 256
+CHUNK = 1024
 
 
 def elu(v):

time: 81.5 us -> 66.5 us (0.82)
  Pallas kernels: 78.6 us -> 63.6 us
    pallas_call x1, Pallas kernels: 41.4 us -> 26.4 us  [local_grads(): pl.pallas_call(local_kernel, out_shape=out, grid_spec=pltpu.PrefetchScala...]
where the time goes in v3:
time: 66.5 us; the launch traced here: 66.3 us
  Pallas kernels  63.6 us (96%)
  local copies, waits for them, and re-layouts  2.12 us (3%)
    pallas_call x1, Pallas kernels, total_panel(): pl.pallas_call(reduce_kernel, out_shape=jax.ShapeDtypeStruct((rows, C), f...  32.5 us
    pallas_call x1, Pallas kernels, local_grads(): pl.pallas_call(local_kernel, out_shape=out, grid_spec=pltpu.PrefetchScala...  26.4 us
    pallas_call x1, Pallas kernels, halos(): pl.pallas_call(halo_kernel, out_shape=[jax.ShapeDtypeStruct(s, jnp.float3...  3.92 us
    unnamed x3, local copies, waits for them, and re-layouts  2.12 us

profile of v3, /device:TPU:29, one launch (start us, length us, event | category | flops | bytes accessed | tf_op | source)
XLA Modules:
  0.0 66.3 jit_solution(5217721822293625479)
XLA Ops:
  0.6 3.9 %shard_map.153 = (f32[2,32,128]{2,1,0:T(8,128)}, f32[2,32,128]{2,1,0:T(8,128)}, f32[2,8,256]{2,1,0:T(8,128)}, f32[2,8,256]{2,1,0:T(8,128)}) custom-call(f32[2,2048,128]{2,1,0:T(8,128)} %x.3, f32[2,1024,256]{2,1,0:T(8,128)} %te.3), custom_call_target="tpu_custom_call" | custom-call | tf_op jit(solution)/shard_map/pallas_call | solution.py:332
  4.6 26.4 %shard_map.154.parts = f32[2,1088,128]{2,1,0:T(8,128)} custom-call(s32[8]{0:T(128)} %starts.1, s32[8]{0:T(128)} %lengths.1, f32[2,2048,128]{2,1,0:T(8,128)} %x.3, f32[2,32,128]{2,1,0:T(8,128)} %get-tuple-element.18.xl, f32[2,32,128]{2,1,0:T(8,128)} %get-tuple-element.19.xr, f32[2,1024,256]{2,1,0:T(8,128)} %te.3, f32[2,8,256]{2,1,0:T(8,128)} %get-tuple-element.20.tl, ...), custom_call_target="tpu_custom_call" | custom-call | tf_op jit(solution)/shard_map/pallas_call | solution.py:221
  30.9 0.0 copy-start
  30.9 1.2 %copy-done = f32[2,1088,128]{2,1,0:T(8,128)S(1)} copy-done((f32[2,1088,128]{2,1,0:T(8,128)S(1)}, f32[2,1088,128]{2,1,0:T(8,128)}, u32[]{:S(2)}) %copy-start) | copy-done | bytes 1114136
  32.2 32.5 %shard_map.155.g = f32[1088,128]{1,0:T(8,128)S(1)} custom-call(f32[2,1088,128]{2,1,0:T(8,128)S(1)} %copy-done), custom_call_target="tpu_custom_call" | custom-call | tf_op jit(solution)/shard_map/pallas_call | solution.py:431
  64.7 0.8 %shard_map.156 = (f32[7,128,64]{2,1,0:T(8,128)S(1)}, f32[1,64]{1,0:T(1,128)}, f32[64,128]{1,0:T(8,128)}, f32[1,64]{1,0:T(1,128)}, f32[4,128,128]{2,1,0:T(8,128)}, /*index=5*/f32[1,128]{1,0:T(1,128)}, f32[1,1]{1,0:T(1,128)}) custom-call(f32[1088,128]{1,0:T(8,128)S(1)} %shard_map.155.g), custom_call_target="tpu_custom_call" | custom-call | tf_op jit(solution)/shard_map/pallas_call | solution.py:468
  65.5 0.9 %copy.17 = f32[7,128,64]{1,2,0:T(8,128)} copy(f32[7,128,64]{2,1,0:T(8,128)S(1)} %get-tuple-element.29) | data formatting | bytes 458752
Async XLA Ops:
  30.9 1.2 %copy-start = (f32[2,1088,128]{2,1,0:T(8,128)S(1)}, f32[2,1088,128]{2,1,0:T(8,128)}, u32[]{:S(2)}) copy-start(f32[2,1088,128]{2,1,0:T(8,128)} %shard_map.154.parts) | copy-start | bytes 3342340
